TPU v7x, 256 devices: a whole 4x4x8 slice. The times are simulated.
256 devices in a mesh: replica: 4 (over x_hi, core), fsdp: 8 (over y, x_lo), tensor: 8 (over z).
Axes of the slice: x: 4 (x_hi: 2, x_lo: 2; x = x_hi * 2 + x_lo), y: 4, z: 8, core: 2. Of those that a mesh axis runs over, the one named last changes fastest.
Arguments:
- partials: bfloat16 [4, 4, 4096, 8192], P('replica', None, 'fsdp', 'tensor'), may hold values from -0.375 to 0.375
- factor_in: float32 [4, 8, 5, 1024, 1024], P('replica', 'tensor', None, None, 'fsdp'), may hold values from -6 to 6
Outputs:
- factor_out: float32 [4, 8, 5, 1024, 1024], P('replica', 'tensor', None, None, 'fsdp')
All inputs are finite; a program needn't handle non-finite values.
Results may differ from a plain program's by a relative error of at most 0.0035.
Values may be sent and summed in bfloat16 or wider, within the bound.
No kernel may reach another device: no remote copies, remote signals or barrier semaphores. Data moves between devices by JAX's collectives and lax.ppermute only.
A program may use at most 128 MiB of HBM per device.

v0:
```python
import jax
import jax.numpy as jnp
from jax import lax
from jax.sharding import PartitionSpec as P


def shifted(value, axis, by):
    peers = lax.axis_size(axis)
    return lax.ppermute(value, axis, [(i, (i + by) % peers) for i in range(peers)])


def cycle_blocks(piece, count):
    blocks = [piece]
    current = piece
    for step in range(1, count):
        current = shifted(current, "tensor", 1)
        blocks.append(current)
    return blocks


def per_device(partials, factor_in):
    received = lax.all_to_all(partials, "replica", split_axis=1, concat_axis=0, tiled=True)
    grad = jnp.sum(received[:, 0].astype(jnp.float32), axis=0).astype(jnp.bfloat16)
    diagonals = factor_in.shape[2]
    blocks = cycle_blocks(grad, diagonals)
    terms = jnp.stack(
        [
            jnp.einsum("mi,mj->ij", grad, other, preferred_element_type=jnp.float32)
            for other in blocks
        ]
    )
    gram = lax.psum_scatter(terms, "fsdp", scatter_dimension=2, tiled=True)
    return 0.9 * factor_in + 0.1 * gram[None, None]


def solution(mesh):
    placed = (P("replica", None, "fsdp", "tensor"), P("replica", "tensor", None, None, "fsdp"))
    return jax.shard_map(
        per_device,
        mesh=mesh,
        in_specs=placed,
        out_specs=P("replica", "tensor", None, None, "fsdp"),
        check_vma=False,
    )
```

profile of v0, /device:TPU:1, one launch (start us, length us, event | category | flops | bytes accessed | tf_op | source)
XLA Modules:
  0.0 588.1 jit_solution(2213519846948497843)
XLA Ops:
  6.5 0.0 reduce-scatter.2.cloned.1.call-start
  6.5 57.5 %all_to_all.4 = bf16[1,4,512,1024]{3,2,0,1:T(8,128)(2,1)} all-to-all(bf16[1,4,512,1024]{3,2,0,1:T(8,128)(2,1)} %bitcast.23), channel_id=1, replica_groups=mesh['replica'=4,'fsdp'=8,'tensor'=8] {'replica'}, dimensions={1} | all-to-all | bytes 8388608 | tf_op jit(solution)/shard_map/all_to_all | solution.py:22
  64.1 3.3 reduce_sum.12
  67.4 0.1 collective-permute-start
  67.5 26.3 %collective-permute-done = bf16[512,1024]{1,0:T(8,128)(2,1)S(1)} collective-permute-done((bf16[512,1024]{1,0:T(8,128)(2,1)S(1)}, bf16[512,1024]{1,0:T(8,128)(2,1)S(1)}, u32[]{:S(2)}, u32[]{:S(2)}) %collective-permute-start) | collective-permute-done | bytes 1048608 | tf_op jit(solution)/shard_map/ppermute | solution.py:9
  93.8 0.0 collective-permute-start.1
  93.8 24.2 %collective-permute-done.1 = bf16[512,1024]{1,0:T(8,128)(2,1)S(1)} collective-permute-done((bf16[512,1024]{1,0:T(8,128)(2,1)S(1)}, bf16[512,1024]{1,0:T(8,128)(2,1)S(1)}, u32[]{:S(2)}, u32[]{:S(2)}) %collective-permute-start.1) | collective-permute-done | bytes 1048608 | tf_op jit(solution)/shard_map/ppermute | solution.py:9
  118.0 0.0 collective-permute-start.2
  118.0 3.2 bitcast_dynamic-update-slice_fusion.4
  121.2 20.1 %collective-permute-done.2 = bf16[512,1024]{1,0:T(8,128)(2,1)S(1)} collective-permute-done((bf16[512,1024]{1,0:T(8,128)(2,1)S(1)}, bf16[512,1024]{1,0:T(8,128)(2,1)S(1)}, u32[]{:S(2)}, u32[]{:S(2)}) %collective-permute-start.2) | collective-permute-done | bytes 1048608 | tf_op jit(solution)/shard_map/ppermute | solution.py:9
  141.3 0.0 collective-permute-start.3
  141.3 3.3 bitcast_dynamic-update-slice_fusion.3
  144.6 3.3 bitcast_dynamic-update-slice_fusion.2
  147.9 3.2 bitcast_dynamic-update-slice_fusion.1
  151.1 12.6 %collective-permute-done.3 = bf16[512,1024]{1,0:T(8,128)(2,1)S(1)} collective-permute-done((bf16[512,1024]{1,0:T(8,128)(2,1)S(1)}, bf16[512,1024]{1,0:T(8,128)(2,1)S(1)}, u32[]{:S(2)}, u32[]{:S(2)}) %collective-permute-start.3) | collective-permute-done | bytes 1048608 | tf_op jit(solution)/shard_map/ppermute | solution.py:9
  163.7 3.2 bitcast_dynamic-update-slice_fusion
  166.9 0.0 copy-start
  166.9 0.0 reduce-scatter.2.cloned.1.call-update
  166.9 410.7 %reduce-scatter.2.cloned.1.call-done = f32[5,1024,128]{2,1,0:T(8,128)} async-done(((f32[5,1024,1024]{2,1,0:T(8,128)}), f32[5,1024,128]{2,1,0:T(8,128)}) %reduce-scatter.2.cloned.1.call-update) | async-done | bytes 2621456 | tf_op jit(solution)/shard_map/reduce_scatter | solution.py:32
  577.6 0.0 copy-done
  577.6 3.6 bitcast_add_fusion
Async XLA Ops:
  6.5 571.1 %reduce-scatter.2.cloned.1.call-start = ((), (), s32[]{:S(2)}) async-start(), calls=%async_computation.2 | async-start | bytes 23592960 | tf_op jit(solution)/shard_map/reduce_scatter | solution.py:32
  67.4 26.4 %collective-permute-start = (bf16[512,1024]{1,0:T(8,128)(2,1)S(1)}, bf16[512,1024]{1,0:T(8,128)(2,1)S(1)}, u32[]{:S(2)}, u32[]{:S(2)}) collective-permute-start(bf16[512,1024]{1,0:T(8,128)(2,1)S(1)} %reduce_sum.12), channel_id=1, source_target_pairs={{0,1},{1,2},{2,3},{3,4},{4,5},{5,6},{6,7},{7,0},{8,9},{9,10},{10,1... | collective-permute-start | bytes 3145736 | tf_op jit(solution)/shard_map/ppermute | solution.py:9
  93.8 24.2 %collective-permute-start.1 = (bf16[512,1024]{1,0:T(8,128)(2,1)S(1)}, bf16[512,1024]{1,0:T(8,128)(2,1)S(1)}, u32[]{:S(2)}, u32[]{:S(2)}) collective-permute-start(bf16[512,1024]{1,0:T(8,128)(2,1)S(1)} %collective-permute-done), channel_id=1, source_target_pairs={{0,1},{1,2},{2,3},{3,4},{4,5},{5,6},{6,7},{7,0},{8,9},{9,10},{10,1... | collective-permute-start | bytes 3145736 | tf_op jit(solution)/shard_map/ppermute | solution.py:9
  118.0 23.3 %collective-permute-start.2 = (bf16[512,1024]{1,0:T(8,128)(2,1)S(1)}, bf16[512,1024]{1,0:T(8,128)(2,1)S(1)}, u32[]{:S(2)}, u32[]{:S(2)}) collective-permute-start(bf16[512,1024]{1,0:T(8,128)(2,1)S(1)} %collective-permute-done.1), channel_id=1, source_target_pairs={{0,1},{1,2},{2,3},{3,4},{4,5},{5,6},{6,7},{7,0},{8,9},{9,10},{10,1... | collective-permute-start | bytes 3145736 | tf_op jit(solution)/shard_map/ppermute | solution.py:9
  141.3 22.4 %collective-permute-start.3 = (bf16[512,1024]{1,0:T(8,128)(2,1)S(1)}, bf16[512,1024]{1,0:T(8,128)(2,1)S(1)}, u32[]{:S(2)}, u32[]{:S(2)}) collective-permute-start(bf16[512,1024]{1,0:T(8,128)(2,1)S(1)} %collective-permute-done.2), channel_id=1, source_target_pairs={{0,1},{1,2},{2,3},{3,4},{4,5},{5,6},{6,7},{7,0},{8,9},{9,10},{10,1... | collective-permute-start | bytes 3145736 | tf_op jit(solution)/shard_map/ppermute | solution.py:9
  166.9 410.7 %copy-start = (f32[1,1,5,1024,128]{4,3,2,1,0:T(8,128)S(1)}, f32[1,1,5,1024,128]{4,3,2,1,0:T(8,128)}, u32[]{:S(2)}) copy-start(f32[1,1,5,1024,128]{4,3,2,1,0:T(8,128)} %param.3) | copy-start | bytes 7864324
Sparse Core Ops, SparseCore 0:
  167.1 410.5 reduce-scatter.1
where the time goes:
time: 588 us
  waiting for transfers between devices  494 us (84%)
  blocking collectives  57.5 us (10%)
  matrix products  16.2 us (3%)
  between operations  13.4 us (2%)
  other arithmetic  6.95 us (1%)
    reduce_scatter x1, waiting for transfers between devices, per_device(): gram = lax.psum_scatter(terms, 'fsdp', scatter_dimension=2, tiled=True)  411 us
    ppermute x4, waiting for transfers between devices, shifted(): lax.ppermute(value, axis, [(i, (i + by) % peers) for i in range(peers)])  83.2 us
    all_to_all x1, blocking collectives, per_device(): lax.all_to_all(partials, 'replica', split_axis=1, concat_axis=0, tiled=True)  57.5 us
    dot_general x5, matrix products, per_device(): jnp.einsum('mi,mj->ij', grad, other, preferred_element_type=jnp.float32)  16.2 us
  transfers between devices with their start and end apart: 5, of which 5 were waited for; matrix products, arithmetic and copies ran while one was open for 2% of the time, Pallas kernels for 0%

commit v1 on v0

v1 whole, which is shorter than its diff:
```python
import jax
import jax.numpy as jnp
from jax import lax
from jax.experimental import pallas as pl
from jax.experimental.pallas import tpu as pltpu
from jax.sharding import PartitionSpec as P

DIMS = (2, 2, 4, 2, 8)
AXES = ("replica", "fsdp", "tensor")
VMEM = 48 * 1024 * 1024


def index_of(xh, core, y, xl, z):
    return (((xh * 2 + core) * 4 + y % 4) * 2 + xl) * 8 + z % 8


def pairs(move):
    out = []
    for xh in range(2):
        for core in range(2):
            for y in range(4):
                for xl in range(2):
                    for z in range(8):
                        out.append((index_of(xh, core, y, xl, z), index_of(*move(xh, core, y, xl, z))))
    return out


def along_x(by):
    def move(xh, core, y, xl, z):
        x = (2 * xh + xl + by) % 4
        return x // 2, core, y, x % 2, z
    return pairs(move)


def along_y(by):
    return pairs(lambda xh, core, y, xl, z: (xh, core, y + by, xl, z))


def along_z(by):
    return pairs(lambda xh, core, y, xl, z: (xh, core, y, xl, z + by))


def to_owner(by):
    return pairs(lambda xh, core, y, xl, z: (xh, xl, y, core, z + by))


SIBLING = pairs(lambda xh, core, y, xl, z: (xh, 1 - core, y, xl, z))


def send(value, where):
    return lax.ppermute(value, AXES, where)


def call(body, grid, ins, outs, shapes, flops=0):
    bytes_accessed = sum(s.size * s.dtype.itemsize for s in jax.tree.leaves(shapes)) * 2
    return pl.pallas_call(
        body,
        grid_spec=pltpu.PrefetchScalarGridSpec(num_scalar_prefetch=1, grid=grid, in_specs=ins, out_specs=outs),
        out_shape=shapes,
        compiler_params=pltpu.CompilerParams(vmem_limit_bytes=VMEM),
        cost_estimate=pl.CostEstimate(flops=flops, bytes_accessed=bytes_accessed, transcendentals=0),
    )


def other_half(partials, where):
    layers, rows, columns = partials.shape

    def body(where_ref, x_ref, o_ref):
        o_ref[...] = x_ref[...]

    return call(
        body, (4,),
        [pl.BlockSpec((layers, rows, 128), lambda q, w: (0, 0, 2 * q + 1 - w[0]))],
        pl.BlockSpec((layers, rows, 128), lambda q, w: (0, 0, q)),
        jax.ShapeDtypeStruct((layers, rows, columns // 2), partials.dtype),
    )(where, partials)


def pair_sums(partials, got, where):
    _, rows, columns = partials.shape

    def body(where_ref, *refs):
        for k in range(3):
            total = refs[2 * k][0].astype(jnp.float32) + refs[2 * k + 1][0].astype(jnp.float32)
            refs[6 + k][...] = total.astype(jnp.bfloat16)

    ins = []
    for k in (1, 2, 3):
        ins.append(pl.BlockSpec((1, rows, 128), lambda q, w, k=k: (lax.rem(w[1] + k, 4), 0, 2 * q + w[0])))
        ins.append(pl.BlockSpec((1, rows, 128), lambda q, w, k=k: (lax.rem(w[1] + k, 4), 0, q)))
    return call(
        body, (4,), ins,
        [pl.BlockSpec((rows, 128), lambda q, w: (0, q))] * 3,
        [jax.ShapeDtypeStruct((rows, columns // 2), jnp.bfloat16)] * 3,
    )(where, *[partials, got] * 3)


def gradient(partials, got, second, left, right, where):
    _, rows, columns = partials.shape

    def body(where_ref, own_ref, got_ref, second_ref, left_ref, right_ref, plain_ref, turned_ref):
        f32 = jnp.float32
        near = own_ref[0].astype(f32) + got_ref[0].astype(f32) + second_ref[...].astype(f32)
        far = left_ref[...].astype(f32) + right_ref[...].astype(f32)
        near, far = near.astype(jnp.bfloat16), far.astype(jnp.bfloat16)
        plain_ref[:rows] = near
        plain_ref[rows:] = far
        turned_ref[:rows] = near
        turned_ref[rows:] = far

    shape = jax.ShapeDtypeStruct((2 * rows, columns // 2), jnp.bfloat16)
    half = pl.BlockSpec((rows, 128), lambda q, w: (0, q))
    return call(
        body, (4,),
        [
            pl.BlockSpec((1, rows, 128), lambda q, w: (w[1], 0, 2 * q + w[0])),
            pl.BlockSpec((1, rows, 128), lambda q, w: (w[1], 0, q)),
            half, half, half,
        ],
        [
            pl.BlockSpec((2 * rows, 128), lambda q, w: (0, q)),
            pl.BlockSpec((2 * rows, 128), lambda q, w: (0, lax.rem(q + 4 - w[2], 4))),
        ],
        [shape, shape],
    )(where, partials, got, second, left, right)


def product(mine, sibling, block, where):
    depth, width = mine.shape

    def body(where_ref, mine_ref, sibling_ref, block_ref, own_ref, *part_refs):
        for k, ref in enumerate((mine_ref, sibling_ref)):
            half = lax.rem(where_ref[0] + k, 2)
            terms = lax.dot_general(ref[...], block_ref[...], (((0,), (0,)), ((), ())), preferred_element_type=jnp.float32)
            for q in range(4):
                rows = pl.ds(pl.multiple_of((2 * q + half) * 128, 128), 128)
                own_ref[rows, :] = terms[q * 128:(q + 1) * 128, :128]
                for j, part_ref in enumerate(part_refs):
                    part_ref[rows, :] = terms[q * 128:(q + 1) * 128, (j + 1) * 128:(j + 2) * 128].astype(jnp.bfloat16)

    whole = pl.BlockSpec((depth, width), lambda i, w: (0, 0))
    part = pl.BlockSpec((2 * width, 128), lambda i, w: (0, 0))
    return call(
        body, (1,),
        [whole, whole, whole],
        [part] * 4,
        [jax.ShapeDtypeStruct((2 * width, 128), jnp.float32)] + [jax.ShapeDtypeStruct((2 * width, 128), jnp.bfloat16)] * 3,
        flops=4 * depth * width * width,
    )(where, mine, sibling, block)


def sum_over_y(parts):
    def joined(j):
        return parts[0][j] if len(parts) == 1 else jnp.concatenate([p[j] for p in parts])

    got = [send(joined(j), along_y(j)) for j in (1, 2, 3)]
    rows = parts[0][0].shape[0]
    sums = []
    for n, part in enumerate(parts):
        total = part[0]
        for piece in got:
            total = total + piece[n * rows:(n + 1) * rows].astype(jnp.float32)
        sums.append(total)
    return sums


def per_device(partials, factor_in):
    replica, fsdp = lax.axis_index("replica"), lax.axis_index("fsdp")
    core, y = replica % 2, fsdp // 2
    x = 2 * (replica // 2) + fsdp % 2
    where = jnp.stack([core, x, y]).astype(jnp.int32)
    partials = partials[0]

    got = send(other_half(partials, where), SIBLING)
    one, two, three = pair_sums(partials, got, where)
    left, second, right = send(one, along_x(1)), send(two, along_x(2)), send(three, along_x(3))
    plain, turned = gradient(partials, got, second, left, right, where)

    up1 = send(turned, along_z(1))
    down1 = send(plain, along_z(-1))
    plain_s = send(plain, SIBLING)
    r0, = sum_over_y([product(plain, plain_s, turned, where)])
    up2 = send(up1, along_z(1))
    down2 = send(down1, along_z(-1))
    down1_s = send(down1, SIBLING)
    r1, r2 = sum_over_y([product(plain, plain_s, up1, where), product(down1, down1_s, up1, where)])
    down2_s = send(down2, SIBLING)
    r3, r4 = sum_over_y([product(down1, down1_s, up2, where), product(down2, down2_s, up2, where)])
    near = send(jnp.concatenate([r0, r1]), to_owner(0))
    grams = [near[:1024], near[1024:], send(r2, to_owner(1)), send(r3, to_owner(1)), send(r4, to_owner(2))]
    return 0.9 * factor_in + 0.1 * jnp.stack(grams)[None, None]


def solution(mesh):
    placed = (P("replica", None, "fsdp", "tensor"), P("replica", "tensor", None, None, "fsdp"))
    return jax.shard_map(
        per_device,
        mesh=mesh,
        in_specs=placed,
        out_specs=P("replica", "tensor", None, None, "fsdp"),
        check_vma=False,
    )
```

time: 588 us -> 185 us (0.31)
  waiting for transfers between devices: 494 us -> 124 us
  blocking collectives: 57.5 us -> 0 us
  starting transfers between devices: 0.09 us -> 36.6 us
  Pallas kernels: 0 us -> 18.7 us
  matrix products: 16.2 us -> 0 us
  between operations: 13.4 us -> 0.24 us
    reduce_scatter x1 -> x0, waiting for transfers between devices: 411 us -> none  [per_device(): gram = lax.psum_scatter(terms, 'fsdp', scatter_dimension=2, tiled=True)]
    all_to_all x1 -> x0, blocking collectives: 57.5 us -> none  [per_device(): lax.all_to_all(partials, 'replica', split_axis=1, concat_axis=0, tiled=True)]
    ppermute x4 -> x24, waiting for transfers between devices: 83.2 us -> 124 us  [send(): return lax.ppermute(value, AXES, where)]
    ppermute x4 -> x24, starting transfers between devices: 0.09 us -> 36.6 us  [send(): return lax.ppermute(value, AXES, where)]
    pallas_call x0 -> x8, Pallas kernels: none -> 18.7 us  [the longest x5 9.08 us: product(): call(body, (1,), [whole, whole, whole], [part] * 4, [jax.ShapeDtypeStruct...]
    dot_general x5 -> x0, matrix products: 16.2 us -> none  [per_device(): jnp.einsum('mi,mj->ij', grad, other, preferred_element_type=jnp.float32)]
  transfers between devices with their start and end apart: 5 -> 24, of which waited for: 5 -> 13; matrix products, arithmetic and copies ran while one was open for 2% -> 1% of each run, Pallas kernels for 0% -> 5%
where the time goes in v1:
time: 185 us; the launch traced here: 183 us
  waiting for transfers between devices  124 us (67%)
  starting transfers between devices  36.6 us (20%)
  Pallas kernels  18.7 us (10%)
  other arithmetic  2.83 us (2%)
    ppermute x24, waiting for transfers between devices, send(): return lax.ppermute(value, AXES, where)  124 us
    ppermute x24, starting transfers between devices, send(): return lax.ppermute(value, AXES, where)  36.6 us
    pallas_call x5, Pallas kernels, product(): call(body, (1,), [whole, whole, whole], [part] * 4, [jax.ShapeDtypeStruct...  9.08 us
  transfers between devices with their start and end apart: 24, of which 13 were waited for; matrix products, arithmetic and copies ran while one was open for 1% of the time, Pallas kernels for 5%

profile of v1, /device:TPU:1, one launch (start us, length us, event | category | flops | bytes accessed | tf_op | source)
XLA Modules:
  0.0 182.6 jit_solution(8859209449809139968)
XLA Ops:
  0.1 3.1 %shard_map.28 = bf16[4,512,512]{2,1,0:T(8,128)(2,1)S(1)} custom-call(s32[3]{0:T(128)S(1)} %pad_add_fusion.where_ref, bf16[4,512,1024]{2,1,0:T(8,128)(2,1)} %bitcast.18), custom_call_target="tpu_custom_call" | custom-call | bytes 4194304 | tf_op jit(solution)/shard_map/pallas_call | solution.py:71
  3.2 3.3 %collective-permute-start = (bf16[4,512,512]{2,1,0:T(8,128)(2,1)S(1)}, bf16[4,512,512]{2,1,0:T(8,128)(2,1)S(1)}, u32[]{:S(2)}, u32[]{:S(2)}) collective-permute-start(bf16[4,512,512]{2,1,0:T(8,128)(2,1)S(1)} %shard_map.28), channel_id=1, source_target_pairs={{0,64},{1,65},{2,66},{3,67},{4,68},{5,69},{6,70},{7,71},{8,72},{9,... | collective-permute-start | bytes 6291464 | tf_op jit(solution)/shard_map/ppermute | solution.py:51
  6.5 3.8 %collective-permute-done.refs_1_.refs_3_.refs_5_.got_ref = bf16[4,512,512]{2,1,0:T(8,128)(2,1)S(1)} collective-permute-done((bf16[4,512,512]{2,1,0:T(8,128)(2,1)S(1)}, bf16[4,512,512]{2,1,0:T(8,128)(2,1)S(1)}, u32[]{:S(2)}, u32[]{:S(2)}) %collective-permute-start) | collective-permute-done | bytes 2097184 | tf_op jit(solution)/shard_map/ppermute | solution.py:51
  10.3 3.4 %shard_map.29 = (bf16[512,512]{1,0:T(8,128)(2,1)S(1)}, bf16[512,512]{1,0:T(8,128)(2,1)S(1)}, bf16[512,512]{1,0:T(8,128)(2,1)S(1)}) custom-call(s32[3]{0:T(128)S(1)} %pad_add_fusion.where_ref, bf16[4,512,1024]{2,1,0:T(8,128)(2,1)} %bitcast.19, bf16[4,512,512]{2,1,0:T(8,128)(2,1)S(1)} %collective-permute-done.refs_1_.refs_3_.refs_5_.got_ref, ...), custom_call_target="tpu_custom_call" | custom-call | bytes 3145728 | tf_op jit(solution)/shard_map/pallas_call | solution.py:91
  15.1 2.4 %collective-permute-start.3 = (bf16[512,512]{1,0:T(8,128)(2,1)S(1)}, bf16[512,512]{1,0:T(8,128)(2,1)S(1)}, u32[]{:S(2)}, u32[]{:S(2)}) collective-permute-start(bf16[512,512]{1,0:T(8,128)(2,1)S(1)} %get-tuple-element.32), channel_id=1, source_target_pairs={{0,136},{1,137},{2,138},{3,139},{4,140},{5,141},{6,142},{7,143},{8... | collective-permute-start | bytes 1572872 | tf_op jit(solution)/shard_map/ppermute | solution.py:51
  17.5 11.0 %collective-permute-done.1.second_ref = bf16[512,512]{1,0:T(8,128)(2,1)S(1)} collective-permute-done((bf16[512,512]{1,0:T(8,128)(2,1)S(1)}, bf16[512,512]{1,0:T(8,128)(2,1)S(1)}, u32[]{:S(2)}, u32[]{:S(2)}) %collective-permute-start.1) | collective-permute-done | bytes 524320 | tf_op jit(solution)/shard_map/ppermute | solution.py:51
  28.5 11.9 %collective-permute-done.2.left_ref = bf16[512,512]{1,0:T(8,128)(2,1)S(1)} collective-permute-done((bf16[512,512]{1,0:T(8,128)(2,1)S(1)}, bf16[512,512]{1,0:T(8,128)(2,1)S(1)}, u32[]{:S(2)}, u32[]{:S(2)}) %collective-permute-start.2) | collective-permute-done | bytes 524320 | tf_op jit(solution)/shard_map/ppermute | solution.py:51
  40.4 3.1 %shard_map.30 = (bf16[1024,512]{1,0:T(8,128)(2,1)S(1)}, bf16[1024,512]{1,0:T(8,128)(2,1)S(1)}) custom-call(s32[3]{0:T(128)S(1)} %pad_add_fusion.where_ref, bf16[4,512,1024]{2,1,0:T(8,128)(2,1)} %bitcast.22, bf16[4,512,512]{2,1,0:T(8,128)(2,1)S(1)} %collective-permute-done.refs_1_.refs_3_.refs_5_.got_ref, ...), custom_call_target="tpu_custom_call" | custom-call | bytes 4194304 | tf_op jit(solution)/shard_map/pallas_call | solution.py:113
  43.5 3.9 %collective-permute-start.9 = (bf16[1024,512]{1,0:T(8,128)(2,1)S(1)}, bf16[1024,512]{1,0:T(8,128)(2,1)S(1)}, u32[]{:S(2)}, u32[]{:S(2)}) collective-permute-start(bf16[1024,512]{1,0:T(8,128)(2,1)S(1)} %get-tuple-element.33.mine_ref), channel_id=1, source_target_pairs={{0,7},{1,0},{2,1},{3,2},{4,3},{5,4},{6,5},{7,6},{8,15},{9,8},{10,9... | collective-permute-start | bytes 3145736 | tf_op jit(solution)/shard_map/ppermute | solution.py:51
  48.3 21.0 %collective-permute-done.9.mine_ref = bf16[1024,512]{1,0:T(8,128)(2,1)S(1)} collective-permute-done((bf16[1024,512]{1,0:T(8,128)(2,1)S(1)}, bf16[1024,512]{1,0:T(8,128)(2,1)S(1)}, u32[]{:S(2)}, u32[]{:S(2)}) %collective-permute-start.9) | collective-permute-done | bytes 1048608 | tf_op jit(solution)/shard_map/ppermute | solution.py:51
  70.8 3.4 %collective-permute-start.17 = (bf16[1024,512]{1,0:T(8,128)(2,1)S(1)}, bf16[1024,512]{1,0:T(8,128)(2,1)S(1)}, u32[]{:S(2)}, u32[]{:S(2)}) collective-permute-start(bf16[1024,512]{1,0:T(8,128)(2,1)S(1)} %collective-permute-done.9.mine_ref), channel_id=1, source_target_pairs={{0,7},{1,0},{2,1},{3,2},{4,3},{5,4},{6,5},{7,6},{8,15},{9,8},{10,9... | collective-permute-start | bytes 3145736 | tf_op jit(solution)/shard_map/ppermute | solution.py:51
  74.2 1.8 shard_map.31
  77.4 2.6 %collective-permute-start.6 = (bf16[1024,128]{1,0:T(8,128)(2,1)S(1)}, bf16[1024,128]{1,0:T(8,128)(2,1)S(1)}, u32[]{:S(2)}, u32[]{:S(2)}) collective-permute-start(bf16[1024,128]{1,0:T(8,128)(2,1)S(1)} %get-tuple-element.37), channel_id=1, source_target_pairs={{0,32},{1,33},{2,34},{3,35},{4,36},{5,37},{6,38},{7,39},{8,40},{9,... | collective-permute-start | bytes 786440 | tf_op jit(solution)/shard_map/ppermute | solution.py:51
  85.7 6.2 %collective-permute-done.6 = bf16[1024,128]{1,0:T(8,128)(2,1)S(1)} collective-permute-done((bf16[1024,128]{1,0:T(8,128)(2,1)S(1)}, bf16[1024,128]{1,0:T(8,128)(2,1)S(1)}, u32[]{:S(2)}, u32[]{:S(2)}) %collective-permute-start.6) | collective-permute-done | bytes 262176 | tf_op jit(solution)/shard_map/ppermute | solution.py:51
  92.2 2.8 %collective-permute-start.13 = (bf16[2048,128]{1,0:T(8,128)(2,1)S(1)}, bf16[2048,128]{1,0:T(8,128)(2,1)S(1)}, u32[]{:S(2)}, u32[]{:S(2)}) collective-permute-start(bf16[2048,128]{1,0:T(8,128)(2,1)S(1)} %pad_maximum_fusion.3), channel_id=1, source_target_pairs={{0,48},{1,49},{2,50},{3,51},{4,52},{5,53},{6,54},{7,55},{8,56},{9,... | collective-permute-start | bytes 1572872 | tf_op jit(solution)/shard_map/ppermute | solution.py:51
  97.7 10.2 %collective-permute-done.16.block_ref = bf16[1024,512]{1,0:T(8,128)(2,1)S(1)} collective-permute-done((bf16[1024,512]{1,0:T(8,128)(2,1)S(1)}, bf16[1024,512]{1,0:T(8,128)(2,1)S(1)}, u32[]{:S(2)}, u32[]{:S(2)}) %collective-permute-start.16) | collective-permute-done | bytes 1048608 | tf_op jit(solution)/shard_map/ppermute | solution.py:51
  109.8 3.6 %collective-permute-done.12 = bf16[2048,128]{1,0:T(8,128)(2,1)S(1)} collective-permute-done((bf16[2048,128]{1,0:T(8,128)(2,1)S(1)}, bf16[2048,128]{1,0:T(8,128)(2,1)S(1)}, u32[]{:S(2)}, u32[]{:S(2)}) %collective-permute-start.12) | collective-permute-done | bytes 524320 | tf_op jit(solution)/shard_map/ppermute | solution.py:51
  113.7 5.0 %collective-permute-start.14 = (f32[2048,128]{1,0:T(8,128)S(1)}, f32[2048,128]{1,0:T(8,128)S(1)}, u32[]{:S(2)}, u32[]{:S(2)}) collective-permute-start(f32[2048,128]{1,0:T(8,128)S(1)} %pad_maximum_fusion), channel_id=1, source_target_pairs={{0,0},{1,1},{2,2},{3,3},{4,4},{5,5},{6,6},{7,7},{8,64},{9,65},{10,... | collective-permute-start | bytes 3145736 | tf_op jit(solution)/shard_map/ppermute | solution.py:51
  118.8 1.8 shard_map.35
  125.3 10.2 %collective-permute-done.19 = bf16[2048,128]{1,0:T(8,128)(2,1)S(1)} collective-permute-done((bf16[2048,128]{1,0:T(8,128)(2,1)S(1)}, bf16[2048,128]{1,0:T(8,128)(2,1)S(1)}, u32[]{:S(2)}, u32[]{:S(2)}) %collective-permute-start.19) | collective-permute-done | bytes 524320 | tf_op jit(solution)/shard_map/ppermute | solution.py:51
  135.6 9.8 %collective-permute-done.20 = bf16[2048,128]{1,0:T(8,128)(2,1)S(1)} collective-permute-done((bf16[2048,128]{1,0:T(8,128)(2,1)S(1)}, bf16[2048,128]{1,0:T(8,128)(2,1)S(1)}, u32[]{:S(2)}, u32[]{:S(2)}) %collective-permute-start.20) | collective-permute-done | bytes 524320 | tf_op jit(solution)/shard_map/ppermute | solution.py:51
  146.9 21.0 %collective-permute-done.22 = f32[1024,128]{1,0:T(8,128)S(1)} collective-permute-done((f32[1024,128]{1,0:T(8,128)S(1)}, f32[1024,128]{1,0:T(8,128)S(1)}, u32[]{:S(2)}, u32[]{:S(2)}) %collective-permute-start.22) | collective-permute-done | bytes 524320 | tf_op jit(solution)/shard_map/ppermute | solution.py:51
  167.9 12.8 %collective-permute-done.23 = f32[1024,128]{1,0:T(8,128)S(1)} collective-permute-done((f32[1024,128]{1,0:T(8,128)S(1)}, f32[1024,128]{1,0:T(8,128)S(1)}, u32[]{:S(2)}, u32[]{:S(2)}) %collective-permute-start.23) | collective-permute-done | bytes 524320 | tf_op jit(solution)/shard_map/ppermute | solution.py:51
  180.7 1.9 %multiply_add_fusion = f32[1,1,5,1024,128]{4,3,2,1,0:T(8,128)} fusion(f32[1,1,5,1024,128]{4,3,2,1,0:T(8,128)S(1)} %bitcast_dynamic-update-slice_fusion, f32[1,1,5,1024,128]{4,3,2,1,0:T(8,128)S(1)} %copy-done), kind=kLoop, calls=%fused_computation | loop fusion | flops 1966080 | bytes 7864320 | tf_op jit(solution)/shard_map/add | solution.py:191
  (51 shorter events, 22.2 us)
Async XLA Ops:
  3.2 7.1 %collective-permute-start = (bf16[4,512,512]{2,1,0:T(8,128)(2,1)S(1)}, bf16[4,512,512]{2,1,0:T(8,128)(2,1)S(1)}, u32[]{:S(2)}, u32[]{:S(2)}) collective-permute-start(bf16[4,512,512]{2,1,0:T(8,128)(2,1)S(1)} %shard_map.28), channel_id=1, source_target_pairs={{0,64},{1,65},{2,66},{3,67},{4,68},{5,69},{6,70},{7,71},{8,72},{9,... | collective-permute-start | bytes 6291464 | tf_op jit(solution)/shard_map/ppermute | solution.py:51
  13.7 14.8 %collective-permute-start.1 = (bf16[512,512]{1,0:T(8,128)(2,1)S(1)}, bf16[512,512]{1,0:T(8,128)(2,1)S(1)}, u32[]{:S(2)}, u32[]{:S(2)}) collective-permute-start(bf16[512,512]{1,0:T(8,128)(2,1)S(1)} %get-tuple-element.30), channel_id=1, source_target_pairs={{0,128},{1,129},{2,130},{3,131},{4,132},{5,133},{6,134},{7,135},{8... | collective-permute-start | bytes 1572872 | tf_op jit(solution)/shard_map/ppermute | solution.py:51
  14.8 25.6 %collective-permute-start.2 = (bf16[512,512]{1,0:T(8,128)(2,1)S(1)}, bf16[512,512]{1,0:T(8,128)(2,1)S(1)}, u32[]{:S(2)}, u32[]{:S(2)}) collective-permute-start(bf16[512,512]{1,0:T(8,128)(2,1)S(1)} %get-tuple-element.31), channel_id=1, source_target_pairs={{0,8},{1,9},{2,10},{3,11},{4,12},{5,13},{6,14},{7,15},{8,128},{9,1... | collective-permute-start | bytes 1572872 | tf_op jit(solution)/shard_map/ppermute | solution.py:51
  15.1 25.3 %collective-permute-start.3 = (bf16[512,512]{1,0:T(8,128)(2,1)S(1)}, bf16[512,512]{1,0:T(8,128)(2,1)S(1)}, u32[]{:S(2)}, u32[]{:S(2)}) collective-permute-start(bf16[512,512]{1,0:T(8,128)(2,1)S(1)} %get-tuple-element.32), channel_id=1, source_target_pairs={{0,136},{1,137},{2,138},{3,139},{4,140},{5,141},{6,142},{7,143},{8... | collective-permute-start | bytes 1572872 | tf_op jit(solution)/shard_map/ppermute | solution.py:51
  43.5 25.8 %collective-permute-start.9 = (bf16[1024,512]{1,0:T(8,128)(2,1)S(1)}, bf16[1024,512]{1,0:T(8,128)(2,1)S(1)}, u32[]{:S(2)}, u32[]{:S(2)}) collective-permute-start(bf16[1024,512]{1,0:T(8,128)(2,1)S(1)} %get-tuple-element.33.mine_ref), channel_id=1, source_target_pairs={{0,7},{1,0},{2,1},{3,2},{4,3},{5,4},{6,5},{7,6},{8,15},{9,8},{10,9... | collective-permute-start | bytes 3145736 | tf_op jit(solution)/shard_map/ppermute | solution.py:51
  47.4 26.8 %collective-permute-start.4 = (bf16[1024,512]{1,0:T(8,128)(2,1)S(1)}, bf16[1024,512]{1,0:T(8,128)(2,1)S(1)}, u32[]{:S(2)}, u32[]{:S(2)}) collective-permute-start(bf16[1024,512]{1,0:T(8,128)(2,1)S(1)} %get-tuple-element.33.mine_ref), channel_id=1, source_target_pairs={{0,64},{1,65},{2,66},{3,67},{4,68},{5,69},{6,70},{7,71},{8,72},{9,... | collective-permute-start | bytes 3145736 | tf_op jit(solution)/shard_map/ppermute | solution.py:51
  48.3 31.7 %collective-permute-start.8 = (bf16[1024,512]{1,0:T(8,128)(2,1)S(1)}, bf16[1024,512]{1,0:T(8,128)(2,1)S(1)}, u32[]{:S(2)}, u32[]{:S(2)}) collective-permute-start(bf16[1024,512]{1,0:T(8,128)(2,1)S(1)} %get-tuple-element.34.block_ref), channel_id=1, source_target_pairs={{0,1},{1,2},{2,3},{3,4},{4,5},{5,6},{6,7},{7,0},{8,9},{9,10},{10,1... | collective-permute-start | bytes 3145736 | tf_op jit(solution)/shard_map/ppermute | solution.py:51
  69.3 13.6 %collective-permute-start.10 = (bf16[1024,512]{1,0:T(8,128)(2,1)S(1)}, bf16[1024,512]{1,0:T(8,128)(2,1)S(1)}, u32[]{:S(2)}, u32[]{:S(2)}) collective-permute-start(bf16[1024,512]{1,0:T(8,128)(2,1)S(1)} %collective-permute-done.9.mine_ref), channel_id=1, source_target_pairs={{0,64},{1,65},{2,66},{3,67},{4,68},{5,69},{6,70},{7,71},{8,72},{9,... | collective-permute-start | bytes 3145736 | tf_op jit(solution)/shard_map/ppermute | solution.py:51
  70.8 26.0 %collective-permute-start.17 = (bf16[1024,512]{1,0:T(8,128)(2,1)S(1)}, bf16[1024,512]{1,0:T(8,128)(2,1)S(1)}, u32[]{:S(2)}, u32[]{:S(2)}) collective-permute-start(bf16[1024,512]{1,0:T(8,128)(2,1)S(1)} %collective-permute-done.9.mine_ref), channel_id=1, source_target_pairs={{0,7},{1,0},{2,1},{3,2},{4,3},{5,4},{6,5},{7,6},{8,15},{9,8},{10,9... | collective-permute-start | bytes 3145736 | tf_op jit(solution)/shard_map/ppermute | solution.py:51
  76.0 9.1 %collective-permute-start.5 = (bf16[1024,128]{1,0:T(8,128)(2,1)S(1)}, bf16[1024,128]{1,0:T(8,128)(2,1)S(1)}, u32[]{:S(2)}, u32[]{:S(2)}) collective-permute-start(bf16[1024,128]{1,0:T(8,128)(2,1)S(1)} %get-tuple-element.36), channel_id=1, source_target_pairs={{0,16},{1,17},{2,18},{3,19},{4,20},{5,21},{6,22},{7,23},{8,24},{9,... | collective-permute-start | bytes 786440 | tf_op jit(solution)/shard_map/ppermute | solution.py:51
  77.4 14.4 %collective-permute-start.6 = (bf16[1024,128]{1,0:T(8,128)(2,1)S(1)}, bf16[1024,128]{1,0:T(8,128)(2,1)S(1)}, u32[]{:S(2)}, u32[]{:S(2)}) collective-permute-start(bf16[1024,128]{1,0:T(8,128)(2,1)S(1)} %get-tuple-element.37), channel_id=1, source_target_pairs={{0,32},{1,33},{2,34},{3,35},{4,36},{5,37},{6,38},{7,39},{8,40},{9,... | collective-permute-start | bytes 786440 | tf_op jit(solution)/shard_map/ppermute | solution.py:51
  80.0 12.2 %collective-permute-start.7 = (bf16[1024,128]{1,0:T(8,128)(2,1)S(1)}, bf16[1024,128]{1,0:T(8,128)(2,1)S(1)}, u32[]{:S(2)}, u32[]{:S(2)}) collective-permute-start(bf16[1024,128]{1,0:T(8,128)(2,1)S(1)} %get-tuple-element.38), channel_id=1, source_target_pairs={{0,48},{1,49},{2,50},{3,51},{4,52},{5,53},{6,54},{7,55},{8,56},{9,... | collective-permute-start | bytes 786440 | tf_op jit(solution)/shard_map/ppermute | solution.py:51
  82.9 25.0 %collective-permute-start.16 = (bf16[1024,512]{1,0:T(8,128)(2,1)S(1)}, bf16[1024,512]{1,0:T(8,128)(2,1)S(1)}, u32[]{:S(2)}, u32[]{:S(2)}) collective-permute-start(bf16[1024,512]{1,0:T(8,128)(2,1)S(1)} %collective-permute-done.8.block_ref), channel_id=1, source_target_pairs={{0,1},{1,2},{2,3},{3,4},{4,5},{5,6},{6,7},{7,0},{8,9},{9,10},{10,1... | collective-permute-start | bytes 3145736 | tf_op jit(solution)/shard_map/ppermute | solution.py:51
  85.2 24.6 %collective-permute-start.11 = (bf16[2048,128]{1,0:T(8,128)(2,1)S(1)}, bf16[2048,128]{1,0:T(8,128)(2,1)S(1)}, u32[]{:S(2)}, u32[]{:S(2)}) collective-permute-start(bf16[2048,128]{1,0:T(8,128)(2,1)S(1)} %pad_maximum_fusion.1), channel_id=1, source_target_pairs={{0,16},{1,17},{2,18},{3,19},{4,20},{5,21},{6,22},{7,23},{8,24},{9,... | collective-permute-start | bytes 1572872 | tf_op jit(solution)/shard_map/ppermute | solution.py:51
  91.9 21.5 %collective-permute-start.12 = (bf16[2048,128]{1,0:T(8,128)(2,1)S(1)}, bf16[2048,128]{1,0:T(8,128)(2,1)S(1)}, u32[]{:S(2)}, u32[]{:S(2)}) collective-permute-start(bf16[2048,128]{1,0:T(8,128)(2,1)S(1)} %pad_maximum_fusion.2), channel_id=1, source_target_pairs={{0,32},{1,33},{2,34},{3,35},{4,36},{5,37},{6,38},{7,39},{8,40},{9,... | collective-permute-start | bytes 1572872 | tf_op jit(solution)/shard_map/ppermute | solution.py:51
  92.2 21.2 %collective-permute-start.13 = (bf16[2048,128]{1,0:T(8,128)(2,1)S(1)}, bf16[2048,128]{1,0:T(8,128)(2,1)S(1)}, u32[]{:S(2)}, u32[]{:S(2)}) collective-permute-start(bf16[2048,128]{1,0:T(8,128)(2,1)S(1)} %pad_maximum_fusion.3), channel_id=1, source_target_pairs={{0,48},{1,49},{2,50},{3,51},{4,52},{5,53},{6,54},{7,55},{8,56},{9,... | collective-permute-start | bytes 1572872 | tf_op jit(solution)/shard_map/ppermute | solution.py:51
  96.8 22.0 %collective-permute-start.18 = (bf16[1024,512]{1,0:T(8,128)(2,1)S(1)}, bf16[1024,512]{1,0:T(8,128)(2,1)S(1)}, u32[]{:S(2)}, u32[]{:S(2)}) collective-permute-start(bf16[1024,512]{1,0:T(8,128)(2,1)S(1)} %collective-permute-done.17.mine_ref), channel_id=1, source_target_pairs={{0,64},{1,65},{2,66},{3,67},{4,68},{5,69},{6,70},{7,71},{8,72},{9,... | collective-permute-start | bytes 3145736 | tf_op jit(solution)/shard_map/ppermute | solution.py:51
  113.7 33.0 %collective-permute-start.14 = (f32[2048,128]{1,0:T(8,128)S(1)}, f32[2048,128]{1,0:T(8,128)S(1)}, u32[]{:S(2)}, u32[]{:S(2)}) collective-permute-start(f32[2048,128]{1,0:T(8,128)S(1)} %pad_maximum_fusion), channel_id=1, source_target_pairs={{0,0},{1,1},{2,2},{3,3},{4,4},{5,5},{6,6},{7,7},{8,64},{9,65},{10,... | collective-permute-start | bytes 3145736 | tf_op jit(solution)/shard_map/ppermute | solution.py:51
  120.7 14.9 %collective-permute-start.19 = (bf16[2048,128]{1,0:T(8,128)(2,1)S(1)}, bf16[2048,128]{1,0:T(8,128)(2,1)S(1)}, u32[]{:S(2)}, u32[]{:S(2)}) collective-permute-start(bf16[2048,128]{1,0:T(8,128)(2,1)S(1)} %pad_maximum_fusion.4), channel_id=1, source_target_pairs={{0,16},{1,17},{2,18},{3,19},{4,20},{5,21},{6,22},{7,23},{8,24},{9,... | collective-permute-start | bytes 1572872 | tf_op jit(solution)/shard_map/ppermute | solution.py:51
  122.4 23.0 %collective-permute-start.20 = (bf16[2048,128]{1,0:T(8,128)(2,1)S(1)}, bf16[2048,128]{1,0:T(8,128)(2,1)S(1)}, u32[]{:S(2)}, u32[]{:S(2)}) collective-permute-start(bf16[2048,128]{1,0:T(8,128)(2,1)S(1)} %pad_maximum_fusion.5), channel_id=1, source_target_pairs={{0,32},{1,33},{2,34},{3,35},{4,36},{5,37},{6,38},{7,39},{8,40},{9,... | collective-permute-start | bytes 1572872 | tf_op jit(solution)/shard_map/ppermute | solution.py:51
  124.0 22.1 %collective-permute-start.21 = (bf16[2048,128]{1,0:T(8,128)(2,1)S(1)}, bf16[2048,128]{1,0:T(8,128)(2,1)S(1)}, u32[]{:S(2)}, u32[]{:S(2)}) collective-permute-start(bf16[2048,128]{1,0:T(8,128)(2,1)S(1)} %pad_maximum_fusion.6), channel_id=1, source_target_pairs={{0,48},{1,49},{2,50},{3,51},{4,52},{5,53},{6,54},{7,55},{8,56},{9,... | collective-permute-start | bytes 1572872 | tf_op jit(solution)/shard_map/ppermute | solution.py:51
  125.3 21.5 %collective-permute-start.15 = (f32[1024,128]{1,0:T(8,128)S(1)}, f32[1024,128]{1,0:T(8,128)S(1)}, u32[]{:S(2)}, u32[]{:S(2)}) collective-permute-start(f32[1024,128]{1,0:T(8,128)S(1)} %get-tuple-element.57), channel_id=1, source_target_pairs={{0,1},{1,2},{2,3},{3,4},{4,5},{5,6},{6,7},{7,0},{8,65},{9,66},{10,... | collective-permute-start | bytes 1572872 | tf_op jit(solution)/shard_map/ppermute | solution.py:51
  146.3 21.6 %collective-permute-start.22 = (f32[1024,128]{1,0:T(8,128)S(1)}, f32[1024,128]{1,0:T(8,128)S(1)}, u32[]{:S(2)}, u32[]{:S(2)}) collective-permute-start(f32[1024,128]{1,0:T(8,128)S(1)} %get-tuple-element.56), channel_id=1, source_target_pairs={{0,1},{1,2},{2,3},{3,4},{4,5},{5,6},{6,7},{7,0},{8,65},{9,66},{10,... | collective-permute-start | bytes 1572872 | tf_op jit(solution)/shard_map/ppermute | solution.py:51
  146.4 34.3 %collective-permute-start.23 = (f32[1024,128]{1,0:T(8,128)S(1)}, f32[1024,128]{1,0:T(8,128)S(1)}, u32[]{:S(2)}, u32[]{:S(2)}) collective-permute-start(f32[1024,128]{1,0:T(8,128)S(1)} %get-tuple-element.55), channel_id=1, source_target_pairs={{0,2},{1,3},{2,4},{3,5},{4,6},{5,7},{6,0},{7,1},{8,66},{9,67},{10,... | collective-permute-start | bytes 1572872 | tf_op jit(solution)/shard_map/ppermute | solution.py:51
  (1 other events, 34.4 us)
